TPU v7x, 256 devices: a whole 4x4x8 slice. The times are simulated.
256 devices in a mesh: dp: 32 (over y, x, core), mp: 8 (over z).
Axes of the slice: x: 4, y: 4, z: 8, core: 2. Of those that a mesh axis runs over, the one named last changes fastest.
Arguments:
- hidden: bfloat16 [768, 256, 4096], P(('dp', 'mp')), may hold values from -6 to 6
- lengths: int32 [768], P(('dp', 'mp')), may hold values from 32 to 256, as said below
- list_ids: int32 [768], P('dp'), may hold values from 0 to 65535, as said below
- gain: bfloat16 [4096], replicated, may hold values from 0.099609375 to 1.8984375
- head: bfloat16 [4096, 1024], P('dp', 'mp'), may hold values from -0.09375 to 0.09375
- list_slot: int32 [65536], replicated, may hold values from 0 to 65535, as said below
- centroids: bfloat16 [65536, 1024], P('dp'), may hold values from -0.59765625 to 0.59765625
- rotation: bfloat16 [1024, 1024], P('mp'), may hold values from -0.1875 to 0.1875
Outputs:
- codes: bfloat16 [768, 1024], P('dp', 'mp')
- scales: bfloat16 [768, 16], P('dp', 'mp')
Inputs may be any that keep to these rules, and one draw needn't show every extreme that they name: `list_ids`: in each aligned block of 24 passages, at most 2 have lists in one range of 2048 lists (list id // 2048); one range holds exactly 2 of them in every block. Each list's row in the centroid table; list_slot[l] // 2048 equals l // 2048, and each row of a range once. `lengths`: some passage has exactly 256 valid tokens.
All inputs are finite; a program needn't handle non-finite values. Where the computation divides by a largest or mean magnitude, that divisor is 1e-20 or more.
Results may differ from a plain program's by a relative error of at most 0.013.
Values may be sent and summed in bfloat16 or wider, within the bound.
A program may use at most 64 MiB of HBM per device.

v0:
```python
import jax
import jax.numpy as jnp
from jax import lax
from jax.sharding import PartitionSpec as P

BLOCK = 64


def quantize(rotated):
    lead = rotated.shape[:-1]
    width = rotated.shape[-1]
    blocks = rotated.reshape(lead + (width // BLOCK, BLOCK))
    scale = jnp.max(jnp.abs(blocks), axis=-1) + 1e-06
    codes = (blocks / scale[..., None]).reshape(lead + (width,)).astype(jnp.bfloat16)
    return (codes, scale.astype(jnp.bfloat16))


def pick_own(placing, buckets):
    picked = jnp.einsum("poc,oce->pe", placing, buckets, preferred_element_type=jnp.float32)
    return picked.astype(buckets.dtype)


def per_device(hidden, lengths, list_ids, gain, head, list_slot, centroids, rotation):
    passes, slots, width = hidden.shape
    states = hidden.astype(jnp.float32)
    mean_square = jnp.mean(states * states, axis=-1)
    valid = jnp.arange(slots, dtype=jnp.int32)[None, :] < lengths[:, None]
    weights = (
        jnp.where(valid, lax.rsqrt(mean_square + 1e-05), 0.0) / lengths.astype(jnp.float32)[:, None]
    )
    pooled_mine = (jnp.einsum("pl,pld->pd", weights, states) * gain.astype(jnp.float32)).astype(
        jnp.bfloat16
    )
    pooled = lax.all_gather(pooled_mine, "mp", axis=0, tiled=True)
    group = pooled.shape[0]
    col_width = head.shape[1]
    projected = jnp.dot(
        pooled, lax.all_gather(head, "dp", axis=0, tiled=True), preferred_element_type=jnp.float32
    ).astype(jnp.bfloat16)
    owners = lax.axis_size("dp")
    lists_own = centroids.shape[0]
    capacity = max(2, 2 * group // owners)
    col_start = lax.axis_index("mp") * col_width
    cent_cols = lax.dynamic_slice_in_dim(centroids, col_start, col_width, 1)
    owner = list_ids // lists_own
    local_row = list_slot[list_ids] % lists_own
    matches = (owner[:, None] == jnp.arange(owners, dtype=jnp.int32)[None, :]).astype(jnp.int32)
    earlier = jnp.cumsum(matches, axis=0) - matches
    rank = jnp.sum(earlier * matches, axis=1)
    placed = (matches[:, :, None] > 0) & (
        rank[:, None, None] == jnp.arange(capacity, dtype=jnp.int32)[None, None, :]
    )
    placing = placed.astype(jnp.bfloat16)
    bucket_ids = jnp.sum(jnp.where(placed, local_row[:, None, None], 0), axis=0)
    bucket_rows = jnp.einsum(
        "poc,pe->oce", placing, projected, preferred_element_type=jnp.float32
    ).astype(jnp.bfloat16)
    rows_in = lax.all_to_all(bucket_rows, "dp", split_axis=0, concat_axis=0, tiled=True)
    row_ids = lax.all_to_all(bucket_ids, "dp", split_axis=0, concat_axis=0, tiled=True)
    cents = cent_cols[row_ids]
    resid = (rows_in.astype(jnp.float32) - cents.astype(jnp.float32)).astype(jnp.bfloat16)
    partial_value = jnp.einsum("oke,ef->okf", resid, rotation, preferred_element_type=jnp.float32)
    rotated = lax.psum_scatter(partial_value, "mp", scatter_dimension=2, tiled=True)
    codes_here, scales_here = quantize(rotated)
    codes_back = lax.all_to_all(codes_here, "dp", split_axis=0, concat_axis=0, tiled=True)
    scales_back = lax.all_to_all(scales_here, "dp", split_axis=0, concat_axis=0, tiled=True)
    codes = pick_own(placing, codes_back)
    scales = pick_own(placing, scales_back)
    return (codes, scales)


def solution(mesh):
    in_specs = (
        P(("dp", "mp"), None, None),
        P(("dp", "mp")),
        P("dp"),
        P(),
        P("dp", "mp"),
        P(),
        P("dp", None),
        P("mp", None),
    )
    out_specs = (P("dp", "mp"), P("dp", "mp"))
    return jax.shard_map(
        per_device, mesh=mesh, in_specs=in_specs, out_specs=out_specs, check_vma=False
    )
```

profile of v0, /device:TPU:1, one launch (start us, length us, event | category | flops | bytes accessed | tf_op | source)
XLA Modules:
  0.0 158.9 jit_solution(10304426160158613519)
XLA Ops:
  7.2 0.7 and_select_fusion.2
  8.2 1.7 %gather_fusion = s32[24]{0:T(128)S(1)} fusion(s32[65536]{0:T(1024)} %param.13, s32[1024]{0:T(1024)S(1)} %pad_clamp_fusion.1), kind=kCustom, calls=%fused_computation | custom fusion | bytes 288 | tf_op jit(solution)/shard_map/gather | solution.py:46
  10.0 0.7 copy.26
  10.7 8.6 %all-to-all-start.1 = ((s32[32,1,2]{2,1,0:T(1,128)}), s32[32,1,2]{2,1,0:T(1,128)S(1)}, u32[]{:S(2)}, u32[]{:S(2)}) async-start(s32[32,1,2]{2,1,0:T(1,128)} %copy.26), calls=%async_computation.1 | async-start | bytes 32768 | tf_op jit(solution)/shard_map/all_to_all | solution.py:59
  19.3 0.7 all-gather.3.cloned.1.call-update
  20.0 4.1 %multiply_reduce_fusion = f32[3,256]{1,0:T(4,128)S(1)} fusion(bf16[3,256,4096]{2,1,0:T(8,128)(2,1)} %param.8), kind=kLoop, calls=%fused_computation.2 | loop fusion | flops 9436416 | bytes 6294528 | tf_op jit(solution)/shard_map/reduce_sum | solution.py:26
  24.2 1.1 constant_dynamic-slice_fusion
  25.3 3.7 %fusion.23 = f32[3,1,4096]{2,1,0:T(1,128)S(1)} fusion(bf16[3,256,4096]{2,1,0:T(8,128)(2,1)} %param.8, bf16[3,256,1]{1,0,2:T(4,128)(2,1)S(1)} %divide_bitcast_fusion), kind=kOutput, calls=%fused_computation.41 | convolution fusion | flops 6291456 | bytes 6342144 | tf_op jit(solution)/shard_map/pl,pld->pd/dot_general | solution.py:31
  29.1 22.9 %all-gather = bf16[8,3,4096]{2,1,0:T(4,128)(2,1)S(1)} all-gather(bf16[1,3,4096]{2,1,0:T(4,128)(2,1)S(1)} %fusion.9), channel_id=1, replica_groups=mesh['dp'=32,'mp'=8] {'mp'}, dimensions={0}, use_global_device_ids=true | all-gather | bytes 221184 | tf_op jit(solution)/shard_map/all_gather | solution.py:34
  52.4 21.1 %all-gather.3.cloned.1.call-done = bf16[4096,128]{1,0:T(8,128)(2,1)} async-done(((bf16[128,128]{1,0:T(8,128)(2,1)}), bf16[4096,128]{1,0:T(8,128)(2,1)}) %all-gather.3.cloned.1.call-update) | async-done | bytes 1048592 | tf_op jit(solution)/shard_map/all_gather | solution.py:38
  73.5 1.6 %convolution_convert_fusion = bf16[32,2,128]{2,0,1:T(8,128)(2,1)S(1)} fusion(bf16[24,4096]{1,0:T(8,128)(2,1)S(1)} %reshape.122, bf16[4096,128]{1,0:T(8,128)(2,1)} %all-gather.3.cloned.1.call-done, pred[24,2]{0,1:T(4,128)(4,1)S(1)} %iota_compare_fusion.2, pred[24,32]{1,0:T(8,128)(4,1)S(1)} %get-tuple-element.4), kind=kOutput, calls=%fused_computation.3 | convolution fusion | flops 25571840 | bytes 1262384 | tf_op jit(solution)/shard_map/poc,pe->oce/dot_general | solution.py:55
  75.8 5.2 %all-to-all-start = ((bf16[32,2,128]{2,1,0:T(2,128)(2,1)}), bf16[32,2,128]{2,1,0:T(2,128)(2,1)S(1)}, u32[]{:S(2)}, u32[]{:S(2)}) async-start(bf16[32,2,128]{2,1,0:T(2,128)(2,1)} %copy.25), calls=%async_computation | async-start | bytes 32768 | tf_op jit(solution)/shard_map/all_to_all | solution.py:58
  81.7 6.2 %all-to-all-done = bf16[32,2,128]{2,1,0:T(2,128)(2,1)S(1)} async-done(((bf16[32,2,128]{2,1,0:T(2,128)(2,1)}), bf16[32,2,128]{2,1,0:T(2,128)(2,1)S(1)}, u32[]{:S(2)}, u32[]{:S(2)}) %all-to-all-start) | async-done | bytes 16416 | tf_op jit(solution)/shard_map/all_to_all | solution.py:58
  87.9 0.9 fusion.3
  88.8 29.0 %reduce-scatter.2.cloned.1.call-done = f32[32,2,128]{2,0,1:T(8,128)} async-done(((f32[32,2,1024]{2,0,1:T(8,128)}), f32[32,2,128]{2,0,1:T(8,128)}) %reduce-scatter.2.cloned.1.call-update) | async-done | bytes 32784 | tf_op jit(solution)/shard_map/reduce_scatter | solution.py:63
  117.9 0.8 abs.6
  119.3 0.7 copy.34
  120.0 13.1 %all-to-all-start.3 = ((bf16[32,2,2]{2,1,0:T(2,128)(2,1)}), bf16[32,2,2]{2,1,0:T(2,128)(2,1)S(1)}, u32[]{:S(2)}, u32[]{:S(2)}) async-start(bf16[32,2,2]{2,1,0:T(2,128)(2,1)} %copy.34), calls=%async_computation.4 | async-start | bytes 32768 | tf_op jit(solution)/shard_map/all_to_all | solution.py:66
  133.1 0.8 divide_convert_fusion
  134.5 5.6 %all-to-all-done.3 = bf16[32,2,2]{2,1,0:T(2,128)(2,1)S(1)} async-done(((bf16[32,2,2]{2,1,0:T(2,128)(2,1)}), bf16[32,2,2]{2,1,0:T(2,128)(2,1)S(1)}, u32[]{:S(2)}, u32[]{:S(2)}) %all-to-all-start.3) | async-done | bytes 288 | tf_op jit(solution)/shard_map/all_to_all | solution.py:66
  140.0 4.1 %all-to-all-start.2 = ((bf16[32,2,128]{2,1,0:T(2,128)(2,1)}), bf16[32,2,128]{2,1,0:T(2,128)(2,1)S(1)}, u32[]{:S(2)}, u32[]{:S(2)}) async-start(bf16[32,2,128]{2,1,0:T(2,128)(2,1)} %copy.32), calls=%async_computation.3 | async-start | bytes 32768 | tf_op jit(solution)/shard_map/all_to_all | solution.py:65
  144.1 0.7 fusion.2
  144.9 6.3 %all-to-all-done.2 = bf16[32,2,128]{2,1,0:T(2,128)(2,1)S(1)} async-done(((bf16[32,2,128]{2,1,0:T(2,128)(2,1)}), bf16[32,2,128]{2,1,0:T(2,128)(2,1)S(1)}, u32[]{:S(2)}, u32[]{:S(2)}) %all-to-all-start.2) | async-done | bytes 16416 | tf_op jit(solution)/shard_map/all_to_all | solution.py:65
  151.2 0.8 fusion
  (38 shorter events, 3.7 us)
Async XLA Ops:
  7.2 80.8 %copy-start = (bf16[128,1024]{1,0:T(8,128)(2,1)S(1)}, bf16[128,1024]{1,0:T(8,128)(2,1)}, u32[]{:S(2)}) copy-start(bf16[128,1024]{1,0:T(8,128)(2,1)} %param.15) | copy-start | bytes 786436
  7.2 16.9 %copy-start.2 = (s32[3]{0:T(128)S(1)}, s32[3]{0:T(128)}, u32[]{:S(2)}) copy-start(s32[3]{0:T(128)} %param.9) | copy-start | bytes 40
  7.2 16.9 %copy-start.1 = (bf16[4096]{0:T(1024)(128)(2,1)S(1)}, bf16[4096]{0:T(1024)(128)(2,1)}, u32[]{:S(2)}) copy-start(bf16[4096]{0:T(1024)(128)(2,1)} %param.11) | copy-start | bytes 24580
  10.7 41.5 %all-to-all-start.1 = ((s32[32,1,2]{2,1,0:T(1,128)}), s32[32,1,2]{2,1,0:T(1,128)S(1)}, u32[]{:S(2)}, u32[]{:S(2)}) async-start(s32[32,1,2]{2,1,0:T(1,128)} %copy.26), calls=%async_computation.1 | async-start | bytes 32768 | tf_op jit(solution)/shard_map/all_to_all | solution.py:59
  19.3 54.2 %all-gather.3.cloned.1.call-start = ((), (), s32[]{:S(2)}) async-start(), calls=%async_computation.5 | async-start | bytes 1081344 | tf_op jit(solution)/shard_map/all_gather | solution.py:38
  75.8 12.1 %all-to-all-start = ((bf16[32,2,128]{2,1,0:T(2,128)(2,1)}), bf16[32,2,128]{2,1,0:T(2,128)(2,1)S(1)}, u32[]{:S(2)}, u32[]{:S(2)}) async-start(bf16[32,2,128]{2,1,0:T(2,128)(2,1)} %copy.25), calls=%async_computation | async-start | bytes 32768 | tf_op jit(solution)/shard_map/all_to_all | solution.py:58
  81.0 36.9 %reduce-scatter.2.cloned.1.call-start = ((), (), s32[]{:S(2)}) async-start(), calls=%async_computation.6 | async-start | bytes 294912 | tf_op jit(solution)/shard_map/reduce_scatter | solution.py:63
  120.0 20.0 %all-to-all-start.3 = ((bf16[32,2,2]{2,1,0:T(2,128)(2,1)}), bf16[32,2,2]{2,1,0:T(2,128)(2,1)S(1)}, u32[]{:S(2)}, u32[]{:S(2)}) async-start(bf16[32,2,2]{2,1,0:T(2,128)(2,1)} %copy.34), calls=%async_computation.4 | async-start | bytes 32768 | tf_op jit(solution)/shard_map/all_to_all | solution.py:66
  140.0 11.2 %all-to-all-start.2 = ((bf16[32,2,128]{2,1,0:T(2,128)(2,1)}), bf16[32,2,128]{2,1,0:T(2,128)(2,1)S(1)}, u32[]{:S(2)}, u32[]{:S(2)}) async-start(bf16[32,2,128]{2,1,0:T(2,128)(2,1)} %copy.32), calls=%async_computation.3 | async-start | bytes 32768 | tf_op jit(solution)/shard_map/all_to_all | solution.py:65
Sparse Core Ops, SparseCore 0:
  22.7 50.8 all-gather.2
  89.0 28.8 reduce-scatter.1
where the time goes:
time: 159 us
  waiting for transfers between devices  68.9 us (43%)
  starting transfers between devices  31 us (19%)
  blocking collectives  22.9 us (14%)
  between operations  14.2 us (9%)
  matrix products  7.76 us (5%)
  other arithmetic  7.05 us (4%)
  local copies, waits for them, and re-layouts  6.99 us (4%)
    reduce_scatter x1, waiting for transfers between devices, per_device(): lax.psum_scatter(partial_value, 'mp', scatter_dimension=2, tiled=True)  29 us
    all_gather x1, blocking collectives, per_device(): pooled = lax.all_gather(pooled_mine, 'mp', axis=0, tiled=True)  22.9 us
    all_gather x1, waiting for transfers between devices, per_device(): lax.all_gather(head, 'dp', axis=0, tiled=True)  21.1 us
    all_to_all x1, starting transfers between devices, per_device(): lax.all_to_all(scales_here, 'dp', split_axis=0, concat_axis=0, tiled=True)  13.1 us
    all_to_all x1, starting transfers between devices, per_device(): lax.all_to_all(bucket_ids, 'dp', split_axis=0, concat_axis=0, tiled=True)  8.59 us
    all_to_all x1, waiting for transfers between devices, per_device(): lax.all_to_all(codes_here, 'dp', split_axis=0, concat_axis=0, tiled=True)  6.33 us
    all_to_all x1, waiting for transfers between devices, per_device(): lax.all_to_all(bucket_rows, 'dp', split_axis=0, concat_axis=0, tiled=True)  6.24 us
    all_to_all x1, waiting for transfers between devices, per_device(): lax.all_to_all(scales_here, 'dp', split_axis=0, concat_axis=0, tiled=True)  5.55 us
  transfers between devices with their start and end apart: 6, of which 5 were waited for; matrix products, arithmetic and copies ran while one was open for 8% of the time, Pallas kernels for 0%

commit v1 on v0

v1 whole, which is shorter than its diff:
```python
import jax
import jax.numpy as jnp
from jax import lax
from jax.experimental import pallas as pl
from jax.experimental.pallas import tpu as pltpu
from jax.sharding import PartitionSpec as P

MESH = pl.DeviceIdType.MESH
F32 = jnp.float32
BF16 = jnp.bfloat16
EPS = 1e-05
HALF = 128
NT = (((1,), (1,)), ((), ()))


def iota(shape, axis):
    return lax.broadcasted_iota(jnp.int32, shape, axis)


def kernel(
    hidden, lengths, list_ids, gain, head, list_slot, centroids, rotation,
    codes_ref, scales_ref,
    hid_v, len_v, ids_all, gain_v, hbuf, slot_v, cent_v, rot_v,
    row_send, row_recv, pool_t, pbuf, pool_f, part_send, part_recv,
    sem_loc, sem_hid, s_ids, r_ids, s_row, r_row, s_pool, r_pool,
    s_h1, r_h1, s_h2, r_h2, s_sib, r_sib, s_part, r_part,
):
    g = lax.axis_index("dp")
    m = lax.axis_index("mp")
    core = lax.rem(g, 2)
    x = lax.rem(g // 2, 4)
    y = g // 8
    first = jnp.where(core == 0, x, y)
    second = jnp.where(core == 0, y, x)
    f_mul = 2 + 6 * core
    s_mul = 8 - 6 * core
    sibling = g + 1 - 2 * core

    def local(src, dst, i):
        return pltpu.make_async_copy(src, dst, sem_loc.at[i])

    loads = [
        local(head, hbuf.at[core, second, first], 0),
        local(list_ids, ids_all.at[g], 1),
        local(lengths, len_v, 2),
        local(gain, gain_v, 3),
        local(list_slot.at[g], slot_v, 4),
        local(centroids.at[:, pl.ds(pl.multiple_of(m * 128, 128), 128)], cent_v, 5),
        local(rotation, rot_v, 6),
    ]
    chunks = []
    for p in range(3):
        for h in range(2):
            rows = pl.ds(h * HALF, HALF)
            chunks.append(
                pltpu.make_async_copy(
                    hidden.at[p, rows], hid_v.at[p, rows], sem_hid.at[2 * p + h]
                )
            )
    for c in loads[:4]:
        c.start()
    for c in chunks[:2]:
        c.start()
    for c in loads[4:6]:
        c.start()
    for c in chunks[2:]:
        c.start()
    loads[6].start()

    barrier = pltpu.get_barrier_semaphore()

    def greet_plane(i, carry):
        pl.semaphore_signal(
            barrier, inc=1, device_id=(lax.rem(g + 1 + i, 32), m), device_id_type=MESH
        )
        return carry

    def greet_z(i, carry):
        pl.semaphore_signal(
            barrier, inc=1, device_id=(g, lax.rem(m + 1 + i, 8)), device_id_type=MESH
        )
        return carry

    lax.fori_loop(0, 31, greet_plane, 0)
    lax.fori_loop(0, 7, greet_z, 0)
    loads[0].wait()
    loads[1].wait()
    pl.semaphore_wait(barrier, 38)

    own = hbuf.at[core, second, first]
    for d in range(1, 4):
        f2 = lax.rem(first + d, 4)
        pltpu.make_async_remote_copy(
            own, own, s_h1, r_h1, device_id=(f2 * f_mul + second * s_mul + core, m), device_id_type=MESH
        ).start()

    def send_ids(i, carry):
        pltpu.make_async_remote_copy(
            ids_all.at[g], ids_all.at[g], s_ids, r_ids,
            device_id=(lax.rem(g + 1 + i, 32), m), device_id_type=MESH,
        ).start()
        return carry

    lax.fori_loop(0, 31, send_ids, 0)
    loads[2].wait()
    loads[3].wait()
    gain_f = gain_v[...].astype(F32)
    ones = jnp.ones((8, 128), BF16)

    def pool(p):
        total = jnp.zeros((8, 4096), F32)
        length = len_v[:, p : p + 1]
        for h in range(2):
            chunks[2 * p + h].wait()
            rows = pl.ds(h * HALF, HALF)
            acc = jnp.zeros((HALF, 128), F32)
            for c in range(32):
                v = hid_v[p, rows, c * 128 : (c + 1) * 128].astype(F32)
                acc += v * v
            hi = acc.astype(BF16)
            lo = (acc - hi.astype(F32)).astype(BF16)
            square = lax.dot_general(ones, hi, NT, preferred_element_type=F32)
            square += lax.dot_general(ones, lo, NT, preferred_element_type=F32)
            token = iota((8, HALF), 1) + h * HALF
            w = jnp.where(token < length, lax.rsqrt(square * (1.0 / 4096) + EPS), 0.0)
            w = w / length.astype(F32)
            w_hi = w.astype(BF16).astype(F32)
            which = iota((8, HALF), 0)
            lhs = jnp.where(which == 0, w_hi, jnp.where(which == 1, w - w_hi, 0.0)).astype(BF16)
            total += jnp.dot(lhs, hid_v[p, rows, :], preferred_element_type=F32)
        line = total[0:1] + total[1:2]
        for c in range(32):
            pool_t[p, c : c + 1, :] = line[:, c * 128 : (c + 1) * 128]
        pbuf[m, p] = (pool_t[p] * gain_f).astype(BF16)
        mine = pbuf.at[m, p]
        for d in range(1, 8):
            pltpu.make_async_remote_copy(
                mine, mine, s_pool.at[p], r_pool.at[p],
                device_id=(g, lax.rem(m + d, 8)), device_id_type=MESH,
            ).start()

    def wait_many(ref, sem):
        pltpu.make_async_copy(ref, ref, sem).wait()

    pool(0)

    wait_many(hbuf.at[core, 0, pl.ds(0, 3)], r_h1)

    def send_second(d):
        s2 = lax.rem(second + d, 4)
        part = hbuf.at[core, second]
        pltpu.make_async_remote_copy(
            part, part, s_h2, r_h2.at[second],
            device_id=(first * f_mul + s2 * s_mul + core, m), device_id_type=MESH,
        ).start()

    for d in (1, 3, 2):
        send_second(d)

    def to_sibling(s):
        part = hbuf.at[core, s]
        pltpu.make_async_remote_copy(
            part, part, s_sib, r_sib.at[s], device_id=(sibling, m), device_id_type=MESH
        ).start()

    to_sibling(second)

    pool(1)

    wait_many(ids_all.at[pl.ds(0, 31)], r_ids)
    loads[4].wait()
    loads[5].wait()
    ids = ids_all[:, 0, :]
    match = (ids >> 11) == g
    lane = iota(ids.shape, 1).astype(F32)
    low = (ids & 2047).astype(F32)
    lo_lane = jnp.min(jnp.where(match, lane, 1e3), axis=1, keepdims=True)
    hi_lane = jnp.max(jnp.where(match, lane, -1.0), axis=1, keepdims=True)
    v0 = jnp.sum(jnp.where(lane == lo_lane, low, 0.0), axis=1, keepdims=True)
    v1 = jnp.sum(jnp.where(lane == hi_lane, low, 0.0), axis=1, keepdims=True)
    wanted = jnp.concatenate([v0, v1], axis=0)
    column = iota((64, 128), 1).astype(F32)
    found = jnp.zeros((64, 128), F32)
    for c in range(16):
        slots = (slot_v[c : c + 1, :] & 2047).astype(F32)
        found += jnp.where(wanted == column + c * 128.0, slots, 0.0)
    found = jnp.sum(found, axis=1, keepdims=True)
    picked = jnp.zeros((64, 128), F32)
    for c in range(16):
        hot = jnp.where(found == column + c * 128.0, 1.0, 0.0).astype(BF16)
        picked += jnp.dot(hot, cent_v[c * 128 : (c + 1) * 128, :], preferred_element_type=F32)
    row_send[:, 0, :] = picked[:32]
    row_send[:, 1, :] = picked[32:]

    def send_rows(i, carry):
        to = lax.rem(g + 1 + i, 32)
        pltpu.make_async_remote_copy(
            row_send.at[to], row_recv.at[g], s_row, r_row, device_id=(to, m), device_id_type=MESH
        ).start()
        return carry

    lax.fori_loop(0, 31, send_rows, 0)
    row_recv[g] = row_send[g]

    pool(2)

    for d in (1, 3, 2):
        s2 = lax.rem(second + d, 4)
        pltpu.make_async_copy(hbuf.at[core, s2], hbuf.at[core, s2], r_h2.at[s2]).wait()
        to_sibling(s2)

    wait_many(row_recv.at[pl.ds(0, 31)], r_row)
    mine = (ids_all[g] >> 11).astype(F32)
    r24 = iota((24, 24), 0)
    c24 = iota((24, 24), 1)
    along = jnp.broadcast_to(mine, (24, 24))
    owner = jnp.sum(jnp.where(r24 == c24, along, 0.0), axis=1, keepdims=True)
    again = jnp.max(jnp.where((along == owner) & (c24 < r24), 1.0, 0.0), axis=1, keepdims=True)
    which = iota((24, 32), 1).astype(F32)
    here = jnp.where(owner == which, 1.0, 0.0)
    cents = jnp.dot(
        (here * (1.0 - again)).astype(BF16), row_recv[:, 0, :].astype(BF16), preferred_element_type=F32
    )
    cents += jnp.dot(
        (here * again).astype(BF16), row_recv[:, 1, :].astype(BF16), preferred_element_type=F32
    )

    for p in range(3):
        wait_many(pbuf.at[pl.ds(0, 7), p], r_pool.at[p])
    pool_f[...] = pbuf[...].reshape(768, 128).astype(F32)
    for s in range(4):
        pltpu.make_async_copy(hbuf.at[0, s], hbuf.at[0, s], r_sib.at[s]).wait()
    projected = jnp.zeros((24, 128), F32)
    for k in range(2):
        for s in range(4):
            parts = []
            for f in range(4):
                r = (s * 4 + f) * 2 if k == 0 else (f * 4 + s) * 2 + 1
                parts.append(pool_f[pl.ds(r, 24, stride=32), :])
            lhs = jnp.concatenate(parts, axis=1).astype(BF16)
            projected += jnp.dot(lhs, hbuf[k, s].reshape(512, 128), preferred_element_type=F32)
    resid = projected.astype(BF16).astype(F32) - cents
    resid = jnp.concatenate([resid, jnp.zeros((8, 128), F32)], axis=0).astype(BF16)

    loads[6].wait()
    partial = jnp.dot(resid, rot_v[...], preferred_element_type=F32)
    for j in range(8):
        part_send[j] = partial[:, j * 128 : (j + 1) * 128].astype(BF16)
    for d in range(1, 8):
        to = lax.rem(m + d, 8)
        pltpu.make_async_remote_copy(
            part_send.at[to], part_recv.at[m], s_part, r_part, device_id=(g, to), device_id_type=MESH
        ).start()
    part_recv[m] = part_send[m]
    wait_many(part_recv.at[pl.ds(0, 7)], r_part)
    rotated = jnp.sum(part_recv[...].astype(F32), axis=0)[:24]
    size = jnp.abs(rotated)
    left = iota((24, 128), 1) < 64
    s0 = jnp.max(jnp.where(left, size, 0.0), axis=1, keepdims=True) + 1e-06
    s1 = jnp.max(jnp.where(left, 0.0, size), axis=1, keepdims=True) + 1e-06
    codes_ref[...] = (rotated / jnp.where(left, s0, s1)).astype(BF16)
    scales_ref[...] = jnp.where(iota((24, 2), 1) == 0, s0, s1).astype(BF16)

    wait_many(hbuf.at[0, 0, pl.ds(0, 3)], s_h1)
    wait_many(hbuf.at[0, pl.ds(0, 3)], s_h2)
    wait_many(hbuf.at[0], s_sib)
    wait_many(ids_all.at[pl.ds(0, 31)], s_ids)
    wait_many(row_send.at[pl.ds(0, 31)], s_row)
    for p in range(3):
        wait_many(pbuf.at[pl.ds(0, 7), p], s_pool.at[p])
    wait_many(part_send.at[pl.ds(0, 7)], s_part)


def per_device(hidden, lengths, list_ids, gain, head, list_slot, centroids, rotation):
    dma = pltpu.SemaphoreType.DMA
    return pl.pallas_call(
        kernel,
        out_shape=(
            jax.ShapeDtypeStruct((24, 128), BF16),
            jax.ShapeDtypeStruct((24, 2), BF16),
        ),
        in_specs=[pl.BlockSpec(memory_space=pl.ANY)] * 8,
        out_specs=(
            pl.BlockSpec(memory_space=pltpu.VMEM),
            pl.BlockSpec(memory_space=pltpu.VMEM),
        ),
        scratch_shapes=[
            pltpu.VMEM((3, 256, 4096), BF16),
            pltpu.VMEM((1, 3), jnp.int32),
            pltpu.VMEM((32, 1, 24), jnp.int32),
            pltpu.VMEM((32, 128), BF16),
            pltpu.VMEM((2, 4, 4, 128, 128), BF16),
            pltpu.VMEM((16, 128), jnp.int32),
            pltpu.VMEM((2048, 128), BF16),
            pltpu.VMEM((128, 1024), BF16),
            pltpu.VMEM((32, 2, 128), F32),
            pltpu.VMEM((32, 2, 128), F32),
            pltpu.VMEM((3, 32, 128), F32),
            pltpu.VMEM((8, 3, 32, 128), BF16),
            pltpu.VMEM((768, 128), F32),
            pltpu.VMEM((8, 32, 128), BF16),
            pltpu.VMEM((8, 32, 128), BF16),
            dma((7,)), dma((6,)),
            dma, dma,
            dma, dma,
            dma((3,)), dma((3,)),
            dma, dma,
            dma, dma((4,)),
            dma, dma((4,)),
            dma, dma,
        ],
        compiler_params=pltpu.CompilerParams(
            collective_id=0, has_side_effects=True, vmem_limit_bytes=56 * 2**20
        ),
    )(
        hidden,
        lengths.reshape(1, 3),
        list_ids.reshape(1, 24),
        gain.reshape(32, 128),
        head,
        list_slot.reshape(32, 16, 128),
        centroids,
        rotation,
    )


def solution(mesh):
    in_specs = (
        P(("dp", "mp"), None, None),
        P(("dp", "mp")),
        P("dp"),
        P(),
        P("dp", "mp"),
        P(),
        P("dp", None),
        P("mp", None),
    )
    out_specs = (P("dp", "mp"), P("dp", "mp"))
    return jax.shard_map(
        per_device, mesh=mesh, in_specs=in_specs, out_specs=out_specs, check_vma=False
    )
```

time: 159 us -> 32.8 us (0.21)
  waiting for transfers between devices: 68.9 us -> 0 us
  starting transfers between devices: 31 us -> 0 us
  Pallas kernels: 0 us -> 29 us
  blocking collectives: 22.9 us -> 0 us
  between operations: 14.2 us -> 0.64 us
  matrix products: 7.76 us -> 0 us
  other arithmetic: 7.05 us -> 0 us
  local copies, waits for them, and re-layouts: 6.99 us -> 2.57 us
    all_to_all x4 -> x0, starting transfers between devices: 30.9 us -> none  [the longest x1 13.1 us: per_device(): lax.all_to_all(scales_here, 'dp', split_axis=0, concat_axis=0, tiled=True)]
    pallas_call x0 -> x1, Pallas kernels: none -> 29 us  [per_device(): pl.pallas_call(kernel, out_shape=(jax.ShapeDtypeStruct((24, 128), BF16),...]
    reduce_scatter x1 -> x0, waiting for transfers between devices: 29 us -> none  [per_device(): lax.psum_scatter(partial_value, 'mp', scatter_dimension=2, tiled=True)]
    all_gather x1 -> x0, blocking collectives: 22.9 us -> none  [per_device(): pooled = lax.all_gather(pooled_mine, 'mp', axis=0, tiled=True)]
    all_gather x1 -> x0, waiting for transfers between devices: 21.1 us -> none  [per_device(): lax.all_gather(head, 'dp', axis=0, tiled=True)]
    all_to_all x4 -> x0, waiting for transfers between devices: 18.1 us -> none  [the longest x1 6.33 us: per_device(): lax.all_to_all(codes_here, 'dp', split_axis=0, concat_axis=0, tiled=True)]
    dot_general x5 -> x0, matrix products: 7.76 us -> none  [the longest x1 3.71 us: per_device(): jnp.einsum('pl,pld->pd', weights, states) * gain.astype(jnp.float32)]
    reduce_sum x3 -> x0, other arithmetic: 4.36 us -> none  [the longest x1 4.08 us: per_device(): mean_square = jnp.mean(states * states, axis=-1)]
  transfers between devices with their start and end apart: 6 -> 0, of which waited for: 5 -> 0; matrix products, arithmetic and copies ran while one was open for 8% -> 0% of each run, Pallas kernels for 0% -> 0%
where the time goes in v1:
time: 32.8 us; the launch traced here: 32.2 us
  Pallas kernels  29 us (88%)
  local copies, waits for them, and re-layouts  2.57 us (8%)
  between operations  0.64 us (2%)
    pallas_call x1, Pallas kernels, per_device(): pl.pallas_call(kernel, out_shape=(jax.ShapeDtypeStruct((24, 128), BF16),...  29 us
    pallas_call x1, local copies, waits for them, and re-layouts, per_device(): pl.pallas_call(kernel, out_shape=(jax.ShapeDtypeStruct((24, 128), BF16),...  1.28 us
    unnamed x1, local copies, waits for them, and re-layouts  1.28 us

profile of v1, /device:TPU:1, one launch (start us, length us, event | category | flops | bytes accessed | tf_op | source)
XLA Modules:
  0.0 32.2 jit_solution(17956901524730188406)
XLA Ops:
  0.6 29.0 %shard_map.95 = (bf16[24,128]{1,0:T(8,128)(2,1)}, bf16[24,2]{1,0:T(8,128)(2,1)}) custom-call(bf16[3,256,4096]{2,1,0:T(8,128)(2,1)} %hidden.1, s32[1,3]{1,0:T(1,128)} %bitcast.6, s32[1,24]{1,0:T(1,128)} %bitcast.7, bf16[32,128]{1,0:T(8,128)(2,1)} %bitcast.5, bf16[128,128]{1,0:T(8,128)(2,1)} %head.1, s32[32,16,128]{2,1,0:T(8,128)} %bitcast.4, ...), custom_call_target="tpu_custom_call" | custom-call | tf_op jit(solution)/shard_map/pallas_call | solution.py:276
  29.7 1.3 %copy.10 = bf16[24,2]{0,1:T(2,128)(2,1)} copy(bf16[24,2]{1,0:T(8,128)(2,1)} %get-tuple-element.3) | data formatting | bytes 192 | tf_op jit(solution)/shard_map/pallas_call | solution.py:276
  31.0 1.3 %copy.12 = bf16[24,128]{1,0:T(8,128)(2,1)} copy(bf16[24,128]{1,0:T(8,128)(2,1)} %get-tuple-element.6) | data formatting | bytes 12288

commit v2 on v1

v2 whole, which is shorter than its diff:
```python
import jax
import jax.numpy as jnp
from jax import lax
from jax.experimental import pallas as pl
from jax.experimental.pallas import tpu as pltpu
from jax.sharding import PartitionSpec as P

MESH = pl.DeviceIdType.MESH
F32 = jnp.float32
BF16 = jnp.bfloat16
EPS = 1e-05
HALF = 128
NT = (((1,), (1,)), ((), ()))
Z_ORDER = (4, 3, 5, 2, 6, 1, 7)
AROUND = (2, 1, 3, 0)
PLANE = [(i, j) for i in AROUND for j in AROUND][:-1]
PLANE.sort(key=lambda o: -min(o[0], 4 - o[0]) - min(o[1], 4 - o[1]))


def iota(shape, axis):
    return lax.broadcasted_iota(jnp.int32, shape, axis)


def kernel(
    hidden, lengths, list_ids, gain, head, list_slot, centroids, rotation,
    rot_ref,
    hid_v, len_v, ids_all, gain_v, hbuf, slot_v, cent_v, rot_v,
    row_f, row_send, row_recv, rcol, pool_t, gain_t, psend, pbuf, pool_f, part_send, part_recv,
    sem_loc, sem_hid, s_ids, r_ids, s_row, r_row, s_pool, r_pool,
    s_head, r_head, s_part, r_part, s_rot, r_rot, s_sib, r_sib,
):
    g = lax.axis_index("dp")
    m = lax.axis_index("mp")
    core = lax.rem(g, 2)
    chip = g // 2
    x = lax.rem(chip, 4)
    y = chip // 4

    def away(dx, dy, k):
        return 2 * (4 * lax.rem(y + dy, 4) + lax.rem(x + dx, 4)) + k

    def local(src, dst, i):
        return pltpu.make_async_copy(src, dst, sem_loc.at[i])

    def remote(src, dst, send, recv, dp, mp):
        return pltpu.make_async_remote_copy(
            src, dst, send, recv, device_id=(dp, mp), device_id_type=MESH
        )

    def wait_many(ref, sem):
        pltpu.make_async_copy(ref, ref, sem).wait()

    loads = [
        local(head, hbuf.at[chip], 0),
        local(list_ids, ids_all.at[g], 1),
        local(lengths, len_v, 2),
        local(gain, gain_v, 3),
        local(list_slot.at[g], slot_v, 4),
        local(centroids, cent_v, 5),
        local(rotation, rot_v, 6),
    ]
    chunks = []
    for p in range(3):
        for h in range(2):
            rows = pl.ds(h * HALF, HALF)
            chunks.append(
                pltpu.make_async_copy(
                    hidden.at[p, rows], hid_v.at[p, rows], sem_hid.at[2 * p + h]
                )
            )
    for c in loads[:4]:
        c.start()
    for c in chunks:
        c.start()
    for c in loads[4:]:
        c.start()

    barrier = pltpu.get_barrier_semaphore()

    def greet_plane(i, carry):
        pl.semaphore_signal(
            barrier, inc=1, device_id=(lax.rem(g + 1 + i, 32), m), device_id_type=MESH
        )
        return carry

    def greet_z(i, carry):
        to = lax.rem(m + 1 + i, 8)
        for k in range(2):
            pl.semaphore_signal(
                barrier, inc=1, device_id=(2 * chip + k, to), device_id_type=MESH
            )
        return carry

    lax.fori_loop(0, 31, greet_plane, 0)
    lax.fori_loop(0, 7, greet_z, 0)

    loads[2].wait()
    loads[3].wait()
    gain_t[...] = gain_v[...].astype(F32)
    ones = jnp.ones((8, 128), BF16)

    def pool(p):
        total = jnp.zeros((8, 4096), F32)
        length = len_v[:, p : p + 1]
        for h in range(2):
            chunks[2 * p + h].wait()
            rows = pl.ds(h * HALF, HALF)
            acc = jnp.zeros((HALF, 128), F32)
            for c in range(32):
                v = hid_v[p, rows, c * 128 : (c + 1) * 128].astype(F32)
                acc += v * v
            hi = acc.astype(BF16)
            lo = (acc - hi.astype(F32)).astype(BF16)
            square = lax.dot_general(ones, hi, NT, preferred_element_type=F32)
            square += lax.dot_general(ones, lo, NT, preferred_element_type=F32)
            token = iota((8, HALF), 1) + h * HALF
            w = jnp.where(token < length, lax.rsqrt(square * (1.0 / 4096) + EPS), 0.0)
            w = w / length.astype(F32)
            w_hi = w.astype(BF16).astype(F32)
            which = iota((8, HALF), 0)
            lhs = jnp.where(which == 0, w_hi, jnp.where(which == 1, w - w_hi, 0.0)).astype(BF16)
            total += jnp.dot(lhs, hid_v[p, rows, :], preferred_element_type=F32)
        line = total[0:1] + total[1:2]
        for c in range(32):
            pool_t[p, c : c + 1, :] = line[:, c * 128 : (c + 1) * 128]
        for k in range(2):
            half = pl.ds(k, 16, stride=2)
            psend[k, p] = (pool_t[p, half, :] * gain_t[half, :]).astype(BF16)

    def send_pooled(first, count, i):
        rows = pl.ds(first, count)
        dst = pbuf.at[core * 8 + m, rows]
        for d in Z_ORDER:
            to = lax.rem(m + d, 8)
            for k in range(2):
                remote(psend.at[k, rows], dst, s_pool.at[i], r_pool.at[i], 2 * chip + k, to).start()
        remote(
            psend.at[1 - core, rows], dst, s_pool.at[i], r_pool.at[i], 2 * chip + 1 - core, m
        ).start()

    pool(0)
    pool(1)
    loads[0].wait()
    loads[1].wait()
    pl.semaphore_wait(barrier, 45)

    mine = ids_all.at[g]
    block = hbuf.at[chip]
    for dx, dy in PLANE:
        for k in range(2):
            remote(mine, mine, s_ids, r_ids, away(dx, dy, k), m).start()
    remote(mine, mine, s_ids, r_ids, 2 * chip + 1 - core, m).start()
    for dx, dy in PLANE:
        remote(block, block, s_head, r_head, away(dx, dy, core), m).start()
    send_pooled(0, 2, 0)
    pool(2)
    send_pooled(2, 1, 1)
    pbuf[core * 8 + m] = psend[core]

    loads[6].wait()
    half = pl.ds(pl.multiple_of(core * 64, 64), 64)

    def columns(j):
        return rot_v.at[half, pl.ds(pl.multiple_of(j * 128, 128), 128)]

    for d in Z_ORDER:
        to = lax.rem(m + d, 8)
        remote(columns(to), rcol.at[core, m], s_rot, r_rot, g, to).start()
    keep = local(columns(m), rcol.at[core, m], 7)
    keep.start()

    loads[4].wait()
    loads[5].wait()
    wait_many(ids_all.at[pl.ds(0, 31)], r_ids)
    ids = ids_all[:, 0, :]
    match = (ids >> 11) == g
    key = (iota(ids.shape, 1) * 2048 + (ids & 2047)).astype(F32)
    k0 = jnp.min(jnp.where(match, key, 1e6), axis=1, keepdims=True)
    k1 = jnp.max(jnp.where(match, key, -1.0), axis=1, keepdims=True)
    wanted = jnp.concatenate([k0, k1], axis=0).astype(jnp.int32) & 2047
    column = iota((64, 128), 1)
    found = jnp.zeros((64, 128), F32)
    for c in range(16):
        slots = (slot_v[c : c + 1, :] & 2047).astype(F32)
        found += jnp.where(wanted == column + c * 128, slots, 0.0)
    found = jnp.sum(found, axis=1, keepdims=True)
    column = column.astype(F32)
    hot = [
        jnp.where(found == column + c * 128.0, 1.0, 0.0).astype(BF16) for c in range(16)
    ]
    picked = jnp.dot(jnp.concatenate(hot, axis=1), cent_v[...], preferred_element_type=F32)
    for r in range(2):
        for c in range(8):
            row_f[pl.ds(8 * r + c, 32, stride=16), :] = picked[
                32 * r : 32 * r + 32, c * 128 : (c + 1) * 128
            ]
    row_send[...] = row_f[...].astype(BF16).reshape(32, 16, 128)
    for dx, dy in PLANE:
        for k in range(2):
            to = away(dx, dy, k)
            remote(row_send.at[to], row_recv.at[g], s_row, r_row, to, m).start()
    to = 2 * chip + 1 - core
    remote(row_send.at[to], row_recv.at[g], s_row, r_row, to, m).start()
    row_recv[g] = row_send[g]

    keep.wait()
    wait_many(rcol.at[0, pl.ds(0, 7)], r_rot)
    remote(rcol.at[core], rcol.at[core], s_sib, r_sib, 2 * chip + 1 - core, m).start()

    mine = (ids_all[g] >> 11).astype(F32)
    r24 = iota((24, 24), 0)
    c24 = iota((24, 24), 1)
    along = jnp.broadcast_to(mine, (24, 24))
    owner = jnp.sum(jnp.where(r24 == c24, along, 0.0), axis=1, keepdims=True)
    again = jnp.max(jnp.where((along == owner) & (c24 < r24), 1.0, 0.0), axis=1, keepdims=True)
    here = jnp.where(owner == iota((24, 32), 1).astype(F32), 1.0, 0.0)
    take = jnp.concatenate([here * (1.0 - again), here * again], axis=1).astype(BF16)

    wait_many(pbuf.at[pl.ds(0, 15), pl.ds(0, 2)], r_pool.at[0])
    wait_many(pbuf.at[pl.ds(0, 15), pl.ds(2, 1)], r_pool.at[1])
    pool_f[...] = pbuf[...].reshape(768, 128).astype(F32)
    lhs = jnp.concatenate([pool_f[pl.ds(c, 48, stride=16), :] for c in range(16)], axis=1)
    lhs = lhs.astype(BF16)
    wait_many(hbuf.at[pl.ds(0, 15)], r_head)
    projected = jnp.dot(lhs, hbuf[...].reshape(2048, 128), preferred_element_type=F32)

    pad = jnp.zeros((8, 128), F32)
    projected = jnp.concatenate([projected[:24], pad, projected[24:], pad], axis=0).astype(BF16)

    partial = jnp.dot(projected, rot_v[...], preferred_element_type=F32)
    for q in range(2):
        for j in range(8):
            part_send[q, j] = partial[32 * q : 32 * q + 32, j * 128 : (j + 1) * 128].astype(BF16)
    dst = part_recv.at[core * 8 + m]
    for d in Z_ORDER:
        to = lax.rem(m + d, 8)
        for q in range(2):
            remote(part_send.at[q, to], dst, s_part, r_part, 2 * chip + q, to).start()
    remote(part_send.at[1 - core, m], dst, s_part, r_part, 2 * chip + 1 - core, m).start()
    part_recv[core * 8 + m] = part_send[core, m]

    wait_many(row_recv.at[pl.ds(0, 31)], r_row)
    row_f[...] = row_recv[...].reshape(512, 128).astype(F32)
    rows = [
        jnp.concatenate(
            [row_f[pl.ds(8 * r + c, 32, stride=16), :] for c in range(8)], axis=1
        )
        for r in range(2)
    ]
    rows = jnp.concatenate(rows, axis=0).astype(BF16)
    cents = jnp.dot(take, rows, preferred_element_type=F32).astype(BF16)
    wait_many(rcol.at[1 - core], r_sib)
    turn = jnp.concatenate([rcol[k, j] for j in range(8) for k in range(2)], axis=0)
    turned = jnp.dot(cents, turn, preferred_element_type=F32)

    wait_many(part_recv.at[pl.ds(0, 15)], r_part)
    rot_ref[...] = jnp.sum(part_recv[...].astype(F32), axis=0)[:24] - turned

    wait_many(hbuf.at[pl.ds(0, 15)], s_head)
    wait_many(ids_all.at[pl.ds(0, 31)], s_ids)
    wait_many(row_send.at[pl.ds(0, 31)], s_row)
    wait_many(pbuf.at[pl.ds(0, 15), pl.ds(0, 2)], s_pool.at[0])
    wait_many(pbuf.at[pl.ds(0, 15), pl.ds(2, 1)], s_pool.at[1])
    wait_many(part_recv.at[pl.ds(0, 15)], s_part)
    wait_many(rcol.at[0, pl.ds(0, 7)], s_rot)
    wait_many(rcol.at[0], s_sib)


def quantize(rot_ref, codes_ref, scales_ref):
    rotated = rot_ref[...]
    size = jnp.abs(rotated)
    left = iota((24, 128), 1) < 64
    s0 = jnp.max(jnp.where(left, size, 0.0), axis=1, keepdims=True) + 1e-06
    s1 = jnp.max(jnp.where(left, 0.0, size), axis=1, keepdims=True) + 1e-06
    codes_ref[...] = (rotated / jnp.where(left, s0, s1)).astype(BF16)
    r24 = iota((24, 24), 0)
    c24 = iota((24, 24), 1)
    s0 = jnp.sum(jnp.where(r24 == c24, s0, 0.0), axis=0, keepdims=True)
    s1 = jnp.sum(jnp.where(r24 == c24, s1, 0.0), axis=0, keepdims=True)
    scales_ref[...] = jnp.concatenate([s0, s1], axis=0).astype(BF16)


def per_device(hidden, lengths, list_ids, gain, head, list_slot, centroids, rotation):
    dma = pltpu.SemaphoreType.DMA
    rotated = pl.pallas_call(
        kernel,
        out_shape=jax.ShapeDtypeStruct((24, 128), F32),
        in_specs=[pl.BlockSpec(memory_space=pl.ANY)] * 8,
        out_specs=pl.BlockSpec(memory_space=pltpu.VMEM),
        scratch_shapes=[
            pltpu.VMEM((3, 256, 4096), BF16),
            pltpu.VMEM((1, 3), jnp.int32),
            pltpu.VMEM((32, 1, 24), jnp.int32),
            pltpu.VMEM((32, 128), BF16),
            pltpu.VMEM((16, 128, 128), BF16),
            pltpu.VMEM((16, 128), jnp.int32),
            pltpu.VMEM((2048, 1024), BF16),
            pltpu.VMEM((128, 1024), BF16),
            pltpu.VMEM((512, 128), F32),
            pltpu.VMEM((32, 16, 128), BF16),
            pltpu.VMEM((32, 16, 128), BF16),
            pltpu.VMEM((2, 8, 64, 128), BF16),
            pltpu.VMEM((3, 32, 128), F32),
            pltpu.VMEM((32, 128), F32),
            pltpu.VMEM((2, 3, 16, 128), BF16),
            pltpu.VMEM((16, 3, 16, 128), BF16),
            pltpu.VMEM((768, 128), F32),
            pltpu.VMEM((2, 8, 32, 128), BF16),
            pltpu.VMEM((16, 32, 128), BF16),
            dma((8,)), dma((6,)),
            dma, dma,
            dma, dma,
            dma((2,)), dma((2,)),
            dma, dma,
            dma, dma,
            dma, dma,
            dma, dma,
        ],
        compiler_params=pltpu.CompilerParams(
            collective_id=0, has_side_effects=True, vmem_limit_bytes=56 * 2**20
        ),
    )(
        hidden,
        lengths.reshape(1, 3),
        list_ids.reshape(1, 24),
        gain.reshape(32, 128),
        head,
        list_slot.reshape(32, 16, 128),
        centroids,
        rotation,
    )
    codes, scales = pl.pallas_call(
        quantize,
        out_shape=(
            jax.ShapeDtypeStruct((24, 128), BF16),
            jax.ShapeDtypeStruct((2, 24), BF16),
        ),
        in_specs=[pl.BlockSpec(memory_space=pltpu.VMEM)],
        out_specs=(
            pl.BlockSpec(memory_space=pltpu.VMEM),
            pl.BlockSpec(memory_space=pltpu.VMEM),
        ),
    )(rotated)
    return codes, scales.T


def solution(mesh):
    in_specs = (
        P(("dp", "mp"), None, None),
        P(("dp", "mp")),
        P("dp"),
        P(),
        P("dp", "mp"),
        P(),
        P("dp", None),
        P("mp", None),
    )
    out_specs = (P("dp", "mp"), P("dp", "mp"))
    return jax.shard_map(
        per_device, mesh=mesh, in_specs=in_specs, out_specs=out_specs, check_vma=False
    )
```

time: 32.8 us -> 29.5 us (0.90); the launches traced: 32.2 us -> 29.4 us
  local copies, waits for them, and re-layouts: 2.57 us -> 0 us
    pallas_call x1 -> x0, local copies, waits for them, and re-layouts: 1.28 us -> none  [per_device(): pl.pallas_call(kernel, out_shape=(jax.ShapeDtypeStruct((24, 128), BF16),...]
    unnamed x1 -> x0, local copies, waits for them, and re-layouts: 1.28 us -> none
    pallas_call x1 -> x2, Pallas kernels: 29 us -> 28.7 us  [the longest x1 27.3 us: per_device(): pl.pallas_call(kernel, out_shape=jax.ShapeDtypeStruct((24, 128), F32), in...]
where the time goes in v2:
time: 29.5 us; the launch traced here: 29.4 us
  Pallas kernels  28.7 us (97%)
  between operations  0.64 us (2%)
    pallas_call x1, Pallas kernels, per_device(): pl.pallas_call(kernel, out_shape=jax.ShapeDtypeStruct((24, 128), F32), in...  27.3 us
    pallas_call x1, Pallas kernels, per_device(): pl.pallas_call(quantize, out_shape=(jax.ShapeDtypeStruct((24, 128), BF16)...  1.39 us

profile of v2, /device:TPU:1, one launch (start us, length us, event | category | flops | bytes accessed | tf_op | source)
XLA Modules:
  0.0 29.4 jit_solution(16080739561460878638)
XLA Ops:
  0.6 27.3 %shard_map.95.rot_ref = f32[24,128]{1,0:T(8,128)} custom-call(bf16[3,256,4096]{2,1,0:T(8,128)(2,1)} %hidden.1, s32[1,3]{1,0:T(1,128)} %bitcast.7, s32[1,24]{1,0:T(1,128)} %bitcast.8, bf16[32,128]{1,0:T(8,128)(2,1)} %bitcast.6, bf16[128,128]{1,0:T(8,128)(2,1)} %head.1, s32[32,16,128]{2,1,0:T(8,128)} %bitcast.5, bf16[2048,1024]{1,0:T(8,128)(2,1)} %centroids.1, ...), custom_call_target="tpu_custom_call" | custom-call | tf_op jit(solution)/shard_map/pallas_call | solution.py:285
  28.0 1.4 %shard_map.96 = (bf16[24,128]{1,0:T(8,128)(2,1)}, bf16[2,24]{1,0:T(2,128)(2,1)}) custom-call(f32[24,128]{1,0:T(8,128)} %shard_map.95.rot_ref), custom_call_target="tpu_custom_call" | custom-call | tf_op jit(solution)/shard_map/pallas_call | solution.py:332

commit v3 on v2

--- a/solution.py
+++ b/solution.py
@@ -14,7 +14,13 @@
 Z_ORDER = (4, 3, 5, 2, 6, 1, 7)
 AROUND = (2, 1, 3, 0)
 PLANE = [(i, j) for i in AROUND for j in AROUND][:-1]
-PLANE.sort(key=lambda o: -min(o[0], 4 - o[0]) - min(o[1], 4 - o[1]))
+
+
+def hops(dx, dy):
+    return min(dx, 4 - dx) + min(dy, 4 - dy)
+
+
+PLANE.sort(key=lambda o: -hops(*o))
 
 
 def iota(shape, axis):
@@ -24,7 +30,7 @@
 def kernel(
     hidden, lengths, list_ids, gain, head, list_slot, centroids, rotation,
     rot_ref,
-    hid_v, len_v, ids_all, gain_v, hbuf, slot_v, cent_v, rot_v,
+    hid_v, len_v, ids_v, ids_all, gain_v, hbuf, slot_v, cent_v, rot_v,
     row_f, row_send, row_recv, rcol, pool_t, gain_t, psend, pbuf, pool_f, part_send, part_recv,
     sem_loc, sem_hid, s_ids, r_ids, s_row, r_row, s_pool, r_pool,
     s_head, r_head, s_part, r_part, s_rot, r_rot, s_sib, r_sib,
@@ -52,10 +58,10 @@
 
     loads = [
         local(head, hbuf.at[chip], 0),
-        local(list_ids, ids_all.at[g], 1),
+        local(list_ids, ids_v, 1),
         local(lengths, len_v, 2),
         local(gain, gain_v, 3),
-        local(list_slot.at[g], slot_v, 4),
+        local(list_slot, slot_v, 4),
         local(centroids, cent_v, 5),
         local(rotation, rot_v, 6),
     ]
@@ -70,91 +76,120 @@
             )
     for c in loads[:4]:
         c.start()
-    for c in chunks:
+    for c in chunks[:2]:
         c.start()
-    for c in loads[4:]:
+    barrier = pltpu.get_barrier_semaphore()
+
+    def greet(dp, mp):
+        pl.semaphore_signal(barrier, inc=1, device_id=(dp, mp), device_id_type=MESH)
+
+    for far in (4, 3, 2, 1):
+        for d in (far, 8 - far)[: 1 if far == 4 else 2]:
+            for k in range(2):
+                greet(2 * chip + k, lax.rem(m + d, 8))
+        for dx, dy in PLANE:
+            if hops(dx, dy) == far:
+                for k in range(2):
+                    greet(away(dx, dy, k), m)
+    greet(2 * chip + 1 - core, m)
+
+    loads[4].start()
+    for c in chunks[2:]:
         c.start()
-
-    barrier = pltpu.get_barrier_semaphore()
-
-    def greet_plane(i, carry):
-        pl.semaphore_signal(
-            barrier, inc=1, device_id=(lax.rem(g + 1 + i, 32), m), device_id_type=MESH
-        )
-        return carry
-
-    def greet_z(i, carry):
-        to = lax.rem(m + 1 + i, 8)
-        for k in range(2):
-            pl.semaphore_signal(
-                barrier, inc=1, device_id=(2 * chip + k, to), device_id_type=MESH
-            )
-        return carry
-
-    lax.fori_loop(0, 31, greet_plane, 0)
-    lax.fori_loop(0, 7, greet_z, 0)
+    for c in loads[5:]:
+        c.start()
 
     loads[2].wait()
     loads[3].wait()
     gain_t[...] = gain_v[...].astype(F32)
     ones = jnp.ones((8, 128), BF16)
 
-    def pool(p):
-        total = jnp.zeros((8, 4096), F32)
+    def weigh(i):
+        p, h = i // 2, i % 2
+        chunks[i].wait()
+        rows = pl.ds(h * HALF, HALF)
         length = len_v[:, p : p + 1]
-        for h in range(2):
-            chunks[2 * p + h].wait()
-            rows = pl.ds(h * HALF, HALF)
-            acc = jnp.zeros((HALF, 128), F32)
-            for c in range(32):
-                v = hid_v[p, rows, c * 128 : (c + 1) * 128].astype(F32)
-                acc += v * v
-            hi = acc.astype(BF16)
-            lo = (acc - hi.astype(F32)).astype(BF16)
-            square = lax.dot_general(ones, hi, NT, preferred_element_type=F32)
-            square += lax.dot_general(ones, lo, NT, preferred_element_type=F32)
-            token = iota((8, HALF), 1) + h * HALF
-            w = jnp.where(token < length, lax.rsqrt(square * (1.0 / 4096) + EPS), 0.0)
-            w = w / length.astype(F32)
-            w_hi = w.astype(BF16).astype(F32)
-            which = iota((8, HALF), 0)
-            lhs = jnp.where(which == 0, w_hi, jnp.where(which == 1, w - w_hi, 0.0)).astype(BF16)
-            total += jnp.dot(lhs, hid_v[p, rows, :], preferred_element_type=F32)
+        acc = jnp.zeros((HALF, 128), F32)
+        for c in range(32):
+            v = hid_v[p, rows, c * 128 : (c + 1) * 128].astype(F32)
+            acc += v * v
+        hi = acc.astype(BF16)
+        lo = (acc - hi.astype(F32)).astype(BF16)
+        square = lax.dot_general(ones, hi, NT, preferred_element_type=F32)
+        square += lax.dot_general(ones, lo, NT, preferred_element_type=F32)
+        token = iota((8, HALF), 1) + h * HALF
+        w = jnp.where(token < length, lax.rsqrt(square * (1.0 / 4096) + EPS), 0.0)
+        w = w / length.astype(F32)
+        w_hi = w.astype(BF16).astype(F32)
+        which = iota((8, HALF), 0)
+        return jnp.where(which == 0, w_hi, jnp.where(which == 1, w - w_hi, 0.0)).astype(BF16)
+
+    def add_up(i, lhs, total):
+        p, h = i // 2, i % 2
+        part = jnp.dot(lhs, hid_v[p, pl.ds(h * HALF, HALF), :], preferred_element_type=F32)
+        if h == 0:
+            return part
+        total = total + part
         line = total[0:1] + total[1:2]
         for c in range(32):
             pool_t[p, c : c + 1, :] = line[:, c * 128 : (c + 1) * 128]
         for k in range(2):
             half = pl.ds(k, 16, stride=2)
             psend[k, p] = (pool_t[p, half, :] * gain_t[half, :]).astype(BF16)
-
-    def send_pooled(first, count, i):
-        rows = pl.ds(first, count)
-        dst = pbuf.at[core * 8 + m, rows]
-        for d in Z_ORDER:
-            to = lax.rem(m + d, 8)
-            for k in range(2):
-                remote(psend.at[k, rows], dst, s_pool.at[i], r_pool.at[i], 2 * chip + k, to).start()
-        remote(
-            psend.at[1 - core, rows], dst, s_pool.at[i], r_pool.at[i], 2 * chip + 1 - core, m
-        ).start()
-
-    pool(0)
-    pool(1)
+        return None
+
+    def pool(first, last, lhs, total):
+        for i in range(first, last):
+            now = weigh(i) if i < 6 else None
+            if i > 0:
+                total = add_up(i - 1, lhs, total)
+            lhs = now
+        return lhs, total
+
+
+    lhs, total = pool(0, 4, None, None)
+
+    loads[1].wait()
+    loads[4].wait()
+    r24 = iota((24, 24), 0)
+    c24 = iota((24, 24), 1)
+
+    def turn(v, axis):
+        return jnp.sum(jnp.where(r24 == c24, v, 0.0), axis=axis, keepdims=True)
+
+    along = jnp.broadcast_to(ids_v[...].astype(F32), (24, 24))
+    ids = turn(along, 1).astype(jnp.int32)
+    table = slot_v[...]
+    hot = jnp.where(iota((24, 512), 1) == (ids >> 7), 1.0, 0.0).astype(BF16)
+    found = 256.0 * jnp.dot(hot, (table >> 8).astype(F32).astype(BF16), preferred_element_type=F32)
+    found += jnp.dot(hot, (table & 255).astype(F32).astype(BF16), preferred_element_type=F32)
+    found = jnp.where(iota((24, 128), 1) == (ids & 127), found, 0.0)
+    slots = jnp.sum(found, axis=1, keepdims=True)
+    ids_all[g] = turn(slots, 0).astype(jnp.int32)
+    owner = (slots.astype(jnp.int32) >> 11).astype(F32)
+    along = jnp.broadcast_to(turn(owner, 0), (24, 24))
+    again = jnp.max(jnp.where((along == owner) & (c24 < r24), 1.0, 0.0), axis=1, keepdims=True)
+    here = jnp.where(owner == iota((24, 32), 1).astype(F32), 1.0, 0.0)
+    take = jnp.concatenate([here * (1.0 - again), here * again], axis=1).astype(BF16)
+
     loads[0].wait()
-    loads[1].wait()
     pl.semaphore_wait(barrier, 45)
 
     mine = ids_all.at[g]
     block = hbuf.at[chip]
+    pooled = pbuf.at[core * 8 + m]
     for dx, dy in PLANE:
         for k in range(2):
             remote(mine, mine, s_ids, r_ids, away(dx, dy, k), m).start()
     remote(mine, mine, s_ids, r_ids, 2 * chip + 1 - core, m).start()
     for dx, dy in PLANE:
         remote(block, block, s_head, r_head, away(dx, dy, core), m).start()
-    send_pooled(0, 2, 0)
-    pool(2)
-    send_pooled(2, 1, 1)
+    pool(4, 7, lhs, total)
+    for d in Z_ORDER:
+        to = lax.rem(m + d, 8)
+        for k in range(2):
+            remote(psend.at[k], pooled, s_pool, r_pool, 2 * chip + k, to).start()
+    remote(psend.at[1 - core], pooled, s_pool, r_pool, 2 * chip + 1 - core, m).start()
     pbuf[core * 8 + m] = psend[core]
 
     loads[6].wait()
@@ -169,7 +204,6 @@
     keep = local(columns(m), rcol.at[core, m], 7)
     keep.start()
 
-    loads[4].wait()
     loads[5].wait()
     wait_many(ids_all.at[pl.ds(0, 31)], r_ids)
     ids = ids_all[:, 0, :]
@@ -179,15 +213,7 @@
     k1 = jnp.max(jnp.where(match, key, -1.0), axis=1, keepdims=True)
     wanted = jnp.concatenate([k0, k1], axis=0).astype(jnp.int32) & 2047
     column = iota((64, 128), 1)
-    found = jnp.zeros((64, 128), F32)
-    for c in range(16):
-        slots = (slot_v[c : c + 1, :] & 2047).astype(F32)
-        found += jnp.where(wanted == column + c * 128, slots, 0.0)
-    found = jnp.sum(found, axis=1, keepdims=True)
-    column = column.astype(F32)
-    hot = [
-        jnp.where(found == column + c * 128.0, 1.0, 0.0).astype(BF16) for c in range(16)
-    ]
+    hot = [jnp.where(wanted == column + c * 128, 1.0, 0.0).astype(BF16) for c in range(16)]
     picked = jnp.dot(jnp.concatenate(hot, axis=1), cent_v[...], preferred_element_type=F32)
     for r in range(2):
         for c in range(8):
@@ -203,21 +229,7 @@
     remote(row_send.at[to], row_recv.at[g], s_row, r_row, to, m).start()
     row_recv[g] = row_send[g]
 
-    keep.wait()
-    wait_many(rcol.at[0, pl.ds(0, 7)], r_rot)
-    remote(rcol.at[core], rcol.at[core], s_sib, r_sib, 2 * chip + 1 - core, m).start()
-
-    mine = (ids_all[g] >> 11).astype(F32)
-    r24 = iota((24, 24), 0)
-    c24 = iota((24, 24), 1)
-    along = jnp.broadcast_to(mine, (24, 24))
-    owner = jnp.sum(jnp.where(r24 == c24, along, 0.0), axis=1, keepdims=True)
-    again = jnp.max(jnp.where((along == owner) & (c24 < r24), 1.0, 0.0), axis=1, keepdims=True)
-    here = jnp.where(owner == iota((24, 32), 1).astype(F32), 1.0, 0.0)
-    take = jnp.concatenate([here * (1.0 - again), here * again], axis=1).astype(BF16)
-
-    wait_many(pbuf.at[pl.ds(0, 15), pl.ds(0, 2)], r_pool.at[0])
-    wait_many(pbuf.at[pl.ds(0, 15), pl.ds(2, 1)], r_pool.at[1])
+    wait_many(pbuf.at[pl.ds(0, 15)], r_pool)
     pool_f[...] = pbuf[...].reshape(768, 128).astype(F32)
     lhs = jnp.concatenate([pool_f[pl.ds(c, 48, stride=16), :] for c in range(16)], axis=1)
     lhs = lhs.astype(BF16)
@@ -239,6 +251,10 @@
     remote(part_send.at[1 - core, m], dst, s_part, r_part, 2 * chip + 1 - core, m).start()
     part_recv[core * 8 + m] = part_send[core, m]
 
+    keep.wait()
+    wait_many(rcol.at[0, pl.ds(0, 7)], r_rot)
+    remote(rcol.at[core], rcol.at[core], s_sib, r_sib, 2 * chip + 1 - core, m).start()
+
     wait_many(row_recv.at[pl.ds(0, 31)], r_row)
     row_f[...] = row_recv[...].reshape(512, 128).astype(F32)
     rows = [
@@ -250,8 +266,8 @@
     rows = jnp.concatenate(rows, axis=0).astype(BF16)
     cents = jnp.dot(take, rows, preferred_element_type=F32).astype(BF16)
     wait_many(rcol.at[1 - core], r_sib)
-    turn = jnp.concatenate([rcol[k, j] for j in range(8) for k in range(2)], axis=0)
-    turned = jnp.dot(cents, turn, preferred_element_type=F32)
+    wheel = jnp.concatenate([rcol[k, j] for j in range(8) for k in range(2)], axis=0)
+    turned = jnp.dot(cents, wheel, preferred_element_type=F32)
 
     wait_many(part_recv.at[pl.ds(0, 15)], r_part)
     rot_ref[...] = jnp.sum(part_recv[...].astype(F32), axis=0)[:24] - turned
@@ -259,8 +275,7 @@
     wait_many(hbuf.at[pl.ds(0, 15)], s_head)
     wait_many(ids_all.at[pl.ds(0, 31)], s_ids)
     wait_many(row_send.at[pl.ds(0, 31)], s_row)
-    wait_many(pbuf.at[pl.ds(0, 15), pl.ds(0, 2)], s_pool.at[0])
-    wait_many(pbuf.at[pl.ds(0, 15), pl.ds(2, 1)], s_pool.at[1])
+    wait_many(pbuf.at[pl.ds(0, 15)], s_pool)
     wait_many(part_recv.at[pl.ds(0, 15)], s_part)
     wait_many(rcol.at[0, pl.ds(0, 7)], s_rot)
     wait_many(rcol.at[0], s_sib)
@@ -290,10 +305,11 @@
         scratch_shapes=[
             pltpu.VMEM((3, 256, 4096), BF16),
             pltpu.VMEM((1, 3), jnp.int32),
+            pltpu.VMEM((1, 24), jnp.int32),
             pltpu.VMEM((32, 1, 24), jnp.int32),
             pltpu.VMEM((32, 128), BF16),
             pltpu.VMEM((16, 128, 128), BF16),
-            pltpu.VMEM((16, 128), jnp.int32),
+            pltpu.VMEM((512, 128), jnp.int32),
             pltpu.VMEM((2048, 1024), BF16),
             pltpu.VMEM((128, 1024), BF16),
             pltpu.VMEM((512, 128), F32),
@@ -310,7 +326,7 @@
             dma((8,)), dma((6,)),
             dma, dma,
             dma, dma,
-            dma((2,)), dma((2,)),
+            dma, dma,
             dma, dma,
             dma, dma,
             dma, dma,
@@ -325,7 +341,7 @@
         list_ids.reshape(1, 24),
         gain.reshape(32, 128),
         head,
-        list_slot.reshape(32, 16, 128),
+        list_slot.reshape(512, 128),
         centroids,
         rotation,
     )

time: 29.5 us -> 28.5 us (0.966)
  Pallas kernels: 28.7 us -> 27.7 us
    pallas_call x1, Pallas kernels: 27.3 us -> 26.3 us  [per_device(): pl.pallas_call(kernel, out_shape=jax.ShapeDtypeStruct((24, 128), F32), in...]
where the time goes in v3:
time: 28.5 us; the launch traced here: 28.3 us
  Pallas kernels  27.7 us (97%)
  between operations  0.64 us (2%)
    pallas_call x1, Pallas kernels, per_device(): pl.pallas_call(kernel, out_shape=jax.ShapeDtypeStruct((24, 128), F32), in...  26.3 us
    pallas_call x1, Pallas kernels, per_device(): pl.pallas_call(quantize, out_shape=(jax.ShapeDtypeStruct((24, 128), BF16)...  1.39 us

profile of v3, /device:TPU:1, one launch (start us, length us, event | category | flops | bytes accessed | tf_op | source)
XLA Modules:
  0.0 28.3 jit_solution(14835956703089428026)
XLA Ops:
  0.6 26.3 %shard_map.95.rot_ref = f32[24,128]{1,0:T(8,128)} custom-call(bf16[3,256,4096]{2,1,0:T(8,128)(2,1)} %hidden.1, s32[1,3]{1,0:T(1,128)} %bitcast.7, s32[1,24]{1,0:T(1,128)} %bitcast.8, bf16[32,128]{1,0:T(8,128)(2,1)} %bitcast.6, bf16[128,128]{1,0:T(8,128)(2,1)} %head.1, s32[512,128]{1,0:T(8,128)} %bitcast.5, bf16[2048,1024]{1,0:T(8,128)(2,1)} %centroids.1, ...), custom_call_target="tpu_custom_call" | custom-call | tf_op jit(solution)/shard_map/pallas_call | solution.py:300
  26.9 1.4 %shard_map.96 = (bf16[24,128]{1,0:T(8,128)(2,1)}, bf16[2,24]{1,0:T(2,128)(2,1)}) custom-call(f32[24,128]{1,0:T(8,128)} %shard_map.95.rot_ref), custom_call_target="tpu_custom_call" | custom-call | tf_op jit(solution)/shard_map/pallas_call | solution.py:348
